TPU v7x, 128 devices: a whole 4x4x4 slice. The times are simulated.
128 devices in a mesh: row: 4 (over y), gz: 2 (over x_lo), vert: 16 (over z, x_hi, core).
Axes of the slice: x: 4 (x_hi: 2, x_lo: 2; x = x_hi * 2 + x_lo), y: 4, z: 4, core: 2. Of those that a mesh axis runs over, the one named last changes fastest.
Arguments:
- distribution: float32 [32, 32, 110592], P('row', 'gz', 'vert'), may hold values from 0 to 10, as said below
- z_order: int32 [48], P('vert'), may hold values from 0 to 47, as said below
- edge_codes: int32 [2, 4], P(None, 'row'), may hold values from 0 to 2, as said below
Outputs:
- new_distribution: float32 [32, 32, 110592], P('row', 'gz', 'vert')
- macroscopic: float32 [8, 32, 32], P(None, 'row', 'gz')
- boundary_flux: float32 [2, 32], P('gz', 'row')
Inputs may be any that keep to these rules, and one draw needn't show every extreme that they name: `z_order`: a permutation of 0 to 47. `edge_codes`: row 0 holds 0 (diffuse wall) or 1 (evaporating film), row 1 holds 0 (diffuse wall) or 2 (outflow); the first column's bottom is film and the last column's top is outflow. `distribution`: every entry is positive.
All inputs are finite; a program needn't handle non-finite values.
Results may differ from a plain program's by a relative error of at most 0.0003.
Values sent between devices are 32-bit elements; how exact they have to be, the bound alone decides.
A program may use at most 128 MiB of HBM per device.

v0:
```python
import math
import jax
import jax.numpy as jnp
import numpy as np
from jax import lax
from jax.sharding import PartitionSpec as P

NODES = 8
NVR = 48
NVT = 48
NVZ = 48
STEPS = 2
ELEMENT_WIDTH = 4.0
TIME_STEP = 0.001
KNUDSEN = 0.005
VISCOUS_RATIO = 2.0 / 3.0
SAT_DENSITY = 1.5
SPEED_LIMIT = 5.0
HIGHEST_PRECISION = lax.Precision.HIGHEST


def with_halo(cells, sides, width):
    for axis, dim in sides:
        count = lax.axis_size(axis)
        ends = count - 1
        head = lax.slice_in_dim(cells, 0, width, axis=dim)
        tail = lax.slice_in_dim(cells, cells.shape[dim] - width, cells.shape[dim], axis=dim)
        cells = jnp.concatenate(
            [
                lax.ppermute(tail, axis, [(i, (i + 1) % count) for i in range(ends)]),
                cells,
                lax.ppermute(head, axis, [((i + 1) % count, i) for i in range(ends)]),
            ],
            axis=dim,
        )
    return cells


def legendre_pair(position, point_count):
    previous = 1.0
    current = position
    for degree in range(2, point_count + 1):
        previous, current = (
            current,
            ((2 * degree - 1) * position * current - (degree - 1) * previous) / degree,
        )
    slope = point_count * (position * current - previous) / (position * position - 1.0)
    return (current, slope)


def dg_tables(point_count):
    point_list = []
    weight_list = []
    for number in range(point_count):
        position = math.cos(math.pi * (number + 0.75) / (point_count + 0.5))
        for sweep in range(60):
            value, slope = legendre_pair(position, point_count)
            position = position - value / slope
        value, slope = legendre_pair(position, point_count)
        point_list.append(position)
        weight_list.append(2.0 / ((1.0 - position * position) * slope * slope))
    point_list = point_list[::-1]
    weight_list = weight_list[::-1]
    products = []
    for row_number in range(point_count):
        product_value = 1.0
        for other in range(point_count):
            if other != row_number:
                product_value = product_value * (point_list[row_number] - point_list[other])
        products.append(product_value)
    derivative_rows = []
    for row_number in range(point_count):
        entries = []
        for column in range(point_count):
            if column == row_number:
                total_value = 0.0
                for other in range(point_count):
                    if other != row_number:
                        total_value = total_value + 1.0 / (
                            point_list[row_number] - point_list[other]
                        )
                entries.append(total_value)
            else:
                entries.append(
                    products[row_number]
                    / products[column]
                    / (point_list[row_number] - point_list[column])
                )
        derivative_rows.append(entries)
    right_list = []
    left_list = []
    for column in range(point_count):
        right_value = 1.0
        left_value = 1.0
        for other in range(point_count):
            if other != column:
                right_value = right_value * (1.0 - point_list[other])
                left_value = left_value * (-1.0 - point_list[other])
        right_list.append(right_value / products[column])
        left_list.append(left_value / products[column])
    points = np.array(point_list)
    quad_weights = np.array(weight_list)
    derivative = np.array(derivative_rows)
    end_right = np.array(right_list)
    end_left = np.array(left_list)
    return (
        points,
        jnp.asarray(derivative, jnp.float32),
        jnp.asarray(end_right / quad_weights, jnp.float32),
        jnp.asarray(end_left / quad_weights, jnp.float32),
        jnp.asarray(end_right, jnp.float32),
        jnp.asarray(end_left, jnp.float32),
    )


def speed_grid(point_count):
    return -SPEED_LIMIT + (np.arange(point_count) + 0.5) * (2.0 * SPEED_LIMIT / point_count)


def shift_velocity(field_entries, offset, keep_mask):
    padding = jnp.zeros(field_entries.shape[:-1] + (abs(offset),), field_entries.dtype)
    if offset > 0:
        shifted = jnp.concatenate([field_entries[..., offset:], padding], -1)
    else:
        shifted = jnp.concatenate([padding, field_entries[..., :offset]], -1)
    return jnp.where(keep_mask, shifted, 0.0)


def on_device(distribution, z_order, edge_codes):
    local_r, local_z, vdev = distribution.shape
    row_count = local_r // NODES
    col_count = local_z // NODES
    node_count = local_r * local_z
    plane_size = NVR * NVT
    slot_count = vdev // plane_size
    row_index = lax.axis_index("row")
    gz_index = lax.axis_index("gz")
    row_total = lax.axis_size("row")
    gz_total = lax.axis_size("gz")
    points, derivative, lift_right, lift_left, end_right, end_left = dg_tables(NODES)
    weight = (
        2
        * SPEED_LIMIT
        / NVR
        * (2 * SPEED_LIMIT / NVT)
        * (2 * SPEED_LIMIT / NVZ)
        / (2 * math.pi) ** 1.5
    )
    grid_r = speed_grid(NVR)
    grid_t = speed_grid(NVT)
    grid_z = speed_grid(NVZ)
    half_flux = float(
        weight
        * np.sum(np.exp(-(grid_r**2) / 2))
        * np.sum(np.exp(-(grid_t**2) / 2))
        * np.sum(np.maximum(grid_z, 0.0) * np.exp(-(grid_z**2) / 2))
    )
    vel_r = jnp.tile(jnp.asarray(np.repeat(grid_r, NVT), jnp.float32), slot_count)
    vel_t = jnp.tile(jnp.asarray(np.tile(grid_t, NVR), jnp.float32), slot_count)
    slot_speeds = jnp.sum(
        jnp.where(
            z_order[:, None] == jnp.arange(NVZ, dtype=jnp.int32)[None, :],
            jnp.asarray(grid_z, jnp.float32)[None, :],
            0.0,
        ),
        1,
    )
    vel_z = jnp.repeat(slot_speeds, plane_size)
    flat_index = jnp.arange(vdev, dtype=jnp.int32)
    a_index = flat_index // NVT % NVR
    b_index = flat_index % NVT
    speed_sq = vel_r**2 + vel_t**2 + vel_z**2
    maxwell_wall = jnp.exp(-speed_sq / 2)
    element_start = (row_index * row_count).astype(jnp.float32)
    radius = (
        (element_start + jnp.arange(row_count, dtype=jnp.float32))[:, None]
        + (1.0 + jnp.asarray(points, jnp.float32))[None, :] / 2
    ) * ELEMENT_WIDTH
    radius = radius.reshape(local_r)
    code_bottom = jnp.repeat(edge_codes[0], NODES)
    code_top = jnp.repeat(edge_codes[1], NODES)
    down_coef = weight * jnp.maximum(-vel_z, 0.0)
    up_coef = weight * jnp.maximum(vel_z, 0.0)

    def gather_moments(current):
        bottom = jnp.einsum("j,rjv->rv", end_left, current[:, :NODES], precision=HIGHEST_PRECISION)
        top_trace = jnp.einsum(
            "j,rjv->rv", end_right, current[:, local_z - NODES :], precision=HIGHEST_PRECISION
        )
        edge_trace = jnp.where(gz_index == 0, bottom, top_trace)
        first_coef = jnp.where(gz_index == 0, down_coef, up_coef)
        bound_sums = jnp.stack(
            [
                jnp.dot(edge_trace, first_coef, precision=HIGHEST_PRECISION),
                jnp.dot(edge_trace, down_coef, precision=HIGHEST_PRECISION),
            ]
        )
        flat = current.reshape(node_count, vdev)
        moment_basis = jnp.stack(
            [
                jnp.full((vdev,), weight, jnp.float32),
                weight * vel_r,
                weight * vel_t,
                weight * vel_z,
                0.5 * weight * speed_sq,
            ],
            1,
        )
        partials = jnp.dot(
            flat, moment_basis, precision=HIGHEST_PRECISION, preferred_element_type=jnp.float32
        )
        integral_sums_table, bound_sums = lax.psum((partials, bound_sums), "vert")
        particle_concentration = integral_sums_table[:, 0]
        bulk_velocity = integral_sums_table[:, 1:4] / particle_concentration[:, None]
        vapour_warmth = (
            2.0 * integral_sums_table[:, 4] / particle_concentration - jnp.sum(bulk_velocity**2, 1)
        ) / 3.0
        thermal_norm_square = (
            (vel_r[None, :] - bulk_velocity[:, 0:1]) ** 2
            + (vel_t[None, :] - bulk_velocity[:, 1:2]) ** 2
            + (vel_z[None, :] - bulk_velocity[:, 2:3]) ** 2
        )
        weighted = flat * thermal_norm_square
        heat_basis = jnp.stack(
            [
                weight * vel_r,
                weight * vel_t,
                weight * vel_z,
                jnp.full((vdev,), weight, jnp.float32),
            ],
            1,
        )
        heat_parts = jnp.dot(
            weighted, heat_basis, precision=HIGHEST_PRECISION, preferred_element_type=jnp.float32
        )
        heat_local = 0.5 * (heat_parts[:, :3] - bulk_velocity * heat_parts[:, 3:4])
        conduction_integral = lax.psum(heat_local, "vert")
        fluid_observables = (
            particle_concentration,
            bulk_velocity[:, 0],
            bulk_velocity[:, 1],
            bulk_velocity[:, 2],
            vapour_warmth,
            conduction_integral[:, 0],
            conduction_integral[:, 1],
            conduction_integral[:, 2],
        )
        fluid_observables = tuple((entry.reshape(local_r, local_z) for entry in fluid_observables))
        return (fluid_observables, bound_sums)

    def advance(current, fluid_observables, bound_sums):
        (
            particle_concentration,
            drift_outward,
            drift_around,
            drift_lengthwise,
            vapour_warmth,
            conduction_outward,
            conduction_around,
            conduction_lengthwise,
        ) = tuple((entry[:, :, None] for entry in fluid_observables))
        grouped = current.reshape(row_count, NODES, local_z, vdev)
        volume = jnp.einsum("ij,ejzv->eizv", derivative, grouped, precision=HIGHEST_PRECISION)
        trace_hi = jnp.einsum("j,ejzv->ezv", end_right, grouped, precision=HIGHEST_PRECISION)
        trace_lo = jnp.einsum("j,ejzv->ezv", end_left, grouped, precision=HIGHEST_PRECISION)
        mirror = (
            trace_lo[0].reshape(local_z, slot_count, NVR, NVT)[:, :, ::-1, :].reshape(local_z, vdev)
        )
        edge_halo = with_halo(jnp.stack([trace_lo[0], trace_hi[-1]]), (("row", 0),), 1)
        from_left = edge_halo[0]
        from_right = edge_halo[3]
        left_ghost = jnp.where(row_index == 0, mirror, from_left)
        right_ghost = jnp.where(row_index == row_total - 1, trace_hi[-1], from_right)
        plus_side = jnp.concatenate([left_ghost[None], trace_hi], 0)
        minus_side = jnp.concatenate([trace_lo, right_ghost[None]], 0)
        face_values = jnp.where(vel_r > 0, plus_side, minus_side)
        radial = (
            2.0
            / ELEMENT_WIDTH
            * vel_r
            * (
                volume
                + lift_right[None, :, None, None] * (face_values[1:] - trace_hi)[:, None]
                - lift_left[None, :, None, None] * (face_values[:-1] - trace_lo)[:, None]
            )
        )
        radial = radial.reshape(local_r, local_z, vdev)
        grouped = current.reshape(local_r, col_count, NODES, vdev)
        volume = jnp.einsum("ij,rejv->reiv", derivative, grouped, precision=HIGHEST_PRECISION)
        trace_hi = jnp.einsum("j,rejv->rev", end_right, grouped, precision=HIGHEST_PRECISION)
        trace_lo = jnp.einsum("j,rejv->rev", end_left, grouped, precision=HIGHEST_PRECISION)
        edge_halo = with_halo(jnp.stack([trace_lo[:, 0], trace_hi[:, -1]]), (("gz", 0),), 1)
        bottom_density = jnp.where(code_bottom == 1, SAT_DENSITY, bound_sums[0] / half_flux)
        top_density = bound_sums[0] / half_flux
        bottom_ghost = bottom_density[:, None] * maxwell_wall[None, :]
        top_ghost = jnp.where(
            code_top[:, None] == 2, trace_hi[:, -1], top_density[:, None] * maxwell_wall[None, :]
        )
        low_ghost = jnp.where(gz_index == 0, bottom_ghost, edge_halo[0])
        high_ghost = jnp.where(gz_index == gz_total - 1, top_ghost, edge_halo[3])
        plus_side = jnp.concatenate([low_ghost[:, None], trace_hi], 1)
        minus_side = jnp.concatenate([trace_lo, high_ghost[:, None]], 1)
        face_values = jnp.where(vel_z > 0, plus_side, minus_side)
        axial_term = (
            2.0
            / ELEMENT_WIDTH
            * vel_z
            * (
                volume
                + lift_right[None, None, :, None] * (face_values[:, 1:] - trace_hi)[:, :, None]
                - lift_left[None, None, :, None] * (face_values[:, :-1] - trace_lo)[:, :, None]
            )
        )
        axial_term = axial_term.reshape(local_r, local_z, vdev)
        step_r = 2 * SPEED_LIMIT / NVR
        step_t = 2 * SPEED_LIMIT / NVT
        grad_r = (
            shift_velocity(current, NVT, a_index < NVR - 1)
            - shift_velocity(current, -NVT, a_index > 0)
        ) / (2 * step_r)
        grad_t = (
            shift_velocity(current, 1, b_index < NVT - 1) - shift_velocity(current, -1, b_index > 0)
        ) / (2 * step_t)
        rotation = (vel_t * vel_t * grad_r - vel_r * vel_t * grad_t) / radius[:, None, None]
        peculiar_r = vel_r - drift_outward
        peculiar_t = vel_t - drift_around
        peculiar_z = vel_z - drift_lengthwise
        thermal_norm_square = peculiar_r**2 + peculiar_t**2 + peculiar_z**2
        projected_conduction = (
            peculiar_r * conduction_outward
            + peculiar_t * conduction_around
            + peculiar_z * conduction_lengthwise
        )
        gaussian_resting_state = (
            particle_concentration
            * vapour_warmth ** (-1.5)
            * jnp.exp(-thermal_norm_square / (2 * vapour_warmth))
        )
        collision_goal_state = gaussian_resting_state * (
            1.0
            + (1.0 - VISCOUS_RATIO)
            * projected_conduction
            / (5.0 * particle_concentration * vapour_warmth**2)
            * (thermal_norm_square / vapour_warmth - 5.0)
        )
        collide = particle_concentration / KNUDSEN * (collision_goal_state - current)
        return current + TIME_STEP * (collide - radial - axial_term - rotation)

    current = distribution
    for step_index in range(STEPS):
        fluid_observables, bound_sums = gather_moments(current)
        current = advance(current, fluid_observables, bound_sums)
    fluid_observables, bound_sums = gather_moments(current)
    macroscopic = jnp.stack(fluid_observables)
    bottom_row = jnp.where(code_bottom == 1, SAT_DENSITY * half_flux - bound_sums[0], 0.0)
    top_row = jnp.where(code_top == 2, bound_sums[0] - bound_sums[1], 0.0)
    boundary_flux = jnp.where(gz_index == 0, bottom_row, top_row)[None]
    return (current, macroscopic, boundary_flux)


def solution(mesh):
    in_specs = (P("row", "gz", "vert"), P("vert"), P(None, "row"))
    out_specs = (P("row", "gz", "vert"), P(None, "row", "gz"), P("gz", "row"))
    return jax.shard_map(
        on_device, mesh=mesh, in_specs=in_specs, out_specs=out_specs, check_vma=False
    )
```

profile of v0, /device:TPU:27, one launch (start us, length us, event | category | flops | bytes accessed | tf_op | source)
XLA Modules:
  0.0 536.6 jit_solution(1569821555901534045)
XLA Ops:
  0.7 5.3 fusion.58
  10.0 5.0 fusion.150
  25.7 5.5 %fusion.148 = f32[1,16,6912]{2,0,1:T(1,128)} fusion(f32[8,1,1]{0,1,2:T(1,128)S(1)} %copy-done.53, f32[8,16,6912]{2,1,0:T(8,128)S(1)} %copy-done), kind=kOutput, calls=%fused_computation.303 | convolution fusion | flops 10616832 | bytes 3981344 | tf_op jit(solution)/shard_map/j,ejzv->ezv/dot_general | solution.py:264
  31.2 4.1 fusion.158
  35.3 4.1 fusion.157
  56.8 4.4 convolution_bitcast_fusion.4
  61.2 35.3 %psum.63 = f32[128,5]{0,1:T(8,128)} all-reduce(f32[128,5]{0,1:T(8,128)} %convolution_bitcast_fusion.4), channel_id=1, replica_groups=mesh['row'=4,'gz'=2,'vert'=16] {'vert'}, use_global_device_ids=true, to_apply=%region_1.2 | all-reduce | flops 640 | bytes 5120 | tf_op jit(solution)/shard_map/psum | solution.py:212
  99.6 4.7 fusion.83
  131.5 37.9 %all-reduce.10 = (f32[2,8]{1,0:T(2,128)}, f32[128,3]{0,1:T(4,128)}) all-reduce(f32[2,8]{1,0:T(2,128)} %pad_maximum_fusion.1, f32[128,3]{0,1:T(4,128)} %subtract_multiply_fusion.14), channel_id=1, replica_groups=mesh['row'=4,'gz'=2,'vert'=16] {'vert'}, use_global_device_ids=true, to_apply=%region_4.5 | all-reduce | flops 400 | bytes 3200 | tf_op jit(solution)/shard_map/psum | solution.py:212
  196.2 4.2 copy.204
  213.7 5.3 collective-permute-done.2
  230.8 14.4 %fusion.23 = f32[8,16,6912]{2,0,1:T(8,128)S(1)} fusion(f32[8,16,6912]{2,0,1:T(8,128)} %bitcast.312, f32[8,8,1]{1,0,2:T(8,128)S(1)} %copy-done.105, f32[8,16,6911]{2,0,1:T(8,128)S(1)} %copy.203, f32[8,16,6911]{2,0,1:T(8,128)S(1)} %copy.204, f32[8,16,6864]{2,0,1:T(8,128)} %copy.205, f32[8,16,6864]{2,0,1:T(8,128)S(1)} %copy.206, f32[8]{0:T(128)S(1)} %add_multiply_fusion, ...), kind=kOutput, calls=%fused_computation.27 | convolution fusion | flops 124747776 | bytes 25806688 | tf_op jit(solution)/shard_map/ij,ejzv->eizv/dot_general | solution.py:263
  253.3 4.3 fusion.164
  270.2 4.1 fusion.154
  293.8 5.4 %fusion.162 = f32[128,5]{0,1:T(8,128)} fusion(f32[128,6912]{1,0:T(8,128)} %bitcast.309, f32[6912,5]{0,1:T(8,128)} %stack.24), kind=kOutput, calls=%fused_computation.317 | convolution fusion | flops 53084160 | bytes 3679744 | tf_op jit(solution)/shard_map/dot_general | solution.py:209
  299.2 35.2 %psum.66 = f32[128,5]{0,1:T(8,128)} all-reduce(f32[128,5]{0,1:T(8,128)} %fusion.162), channel_id=1, replica_groups=mesh['row'=4,'gz'=2,'vert'=16] {'vert'}, use_global_device_ids=true, to_apply=%region_5.6 | all-reduce | flops 640 | bytes 5120 | tf_op jit(solution)/shard_map/psum | solution.py:212
  337.7 5.9 %fusion.73 = f32[128,4]{0,1:T(4,128)S(1)} fusion(f32[128,6912]{1,0:T(8,128)} %bitcast.310, f32[128]{0:T(128)S(1)} %get-tuple-element.110, f32[128]{0:T(128)S(1)} %get-tuple-element.109, f32[128]{0:T(128)S(1)} %get-tuple-element.108, f32[6912]{0:T(1024)} %sub.385, f32[6912]{0:T(1024)} %sub.380, f32[6912]{0:T(1024)} %sub.375, f32[6912,1]{0,1:T(1,128)} %broadcast.609, ...), kind=kOutput, calls=%fused_computation.89 | convolution fusion | flops 50512896 | bytes 3736064 | tf_op jit(solution)/shard_map/dot_general | solution.py:233
  366.7 33.9 %all-reduce.9 = (f32[2,8]{1,0:T(2,128)}, f32[128,3]{0,1:T(4,128)}) all-reduce(f32[2,8]{1,0:T(2,128)} %pad_maximum_fusion.2, f32[128,3]{0,1:T(4,128)} %subtract_multiply_fusion.13), channel_id=1, replica_groups=mesh['row'=4,'gz'=2,'vert'=16] {'vert'}, use_global_device_ids=true, to_apply=%region_8.9 | all-reduce | flops 400 | bytes 3200 | tf_op jit(solution)/shard_map/psum | solution.py:212
  417.3 4.3 collective-permute-done.6
  425.2 4.8 fusion.2
  436.5 11.2 %fusion.18 = f32[8,16,6912]{2,0,1:T(8,128)S(1)} fusion(f32[8,16,6912]{2,0,1:T(8,128)S(1)} %fusion.23, f32[8,16,6912]{2,0,1:T(8,128)} %bitcast.311, f32[8,8,1]{1,0,2:T(8,128)S(1)} %copy-done.106, f32[8,16,6911]{2,0,1:T(8,128)} %get-tuple-element.57, f32[8,16,6911]{2,0,1:T(8,128)S(1)} %copy-done.22, f32[8,16,6864]{2,0,1:T(8,128)S(1)} %copy-done.21, ...), kind=kOutput, calls=%fused_computation.22 | convolution fusion | flops 124747776 | bytes 25806688 | tf_op jit(solution)/shard_map/ij,ejzv->eizv/dot_general | solution.py:263
  457.7 34.3 %psum.69 = f32[128,5]{0,1:T(8,128)S(1)} all-reduce(f32[128,5]{0,1:T(8,128)S(1)} %fusion.165), channel_id=1, replica_groups=mesh['row'=4,'gz'=2,'vert'=16] {'vert'}, use_global_device_ids=true, to_apply=%region_9.10 | all-reduce | flops 640 | bytes 5120 | tf_op jit(solution)/shard_map/psum | solution.py:212
  493.7 4.7 fusion.63
  501.5 33.2 %all-reduce.8 = (f32[128,3]{0,1:T(4,128)S(1)}, f32[2,8]{1,0:T(2,128)S(1)}) all-reduce(f32[128,3]{0,1:T(4,128)S(1)} %subtract_multiply_fusion.12, f32[2,8]{1,0:T(2,128)S(1)} %pad_maximum_fusion.3), channel_id=1, replica_groups=mesh['row'=4,'gz'=2,'vert'=16] {'vert'}, use_global_device_ids=true, to_apply=%region_11.12 | all-reduce | flops 400 | bytes 3200 | tf_op jit(solution)/shard_map/psum | solution.py:237
  (399 shorter events, 220.8 us)
Async XLA Ops:
  7.1 16.4 %copy-start.53 = (f32[8,1,1]{0,1,2:T(1,128)S(1)}, f32[8,1,1]{0,1,2:T(1,128)}, u32[]{:S(2)}) copy-start(f32[8,1,1]{0,1,2:T(1,128)} %constant.165) | copy-start | bytes 100
  7.1 202.2 %collective-permute-start.3 = (f32[1,8,6912]{2,0,1:T(1,128)}, f32[1,8,6912]{2,0,1:T(1,128)}, u32[]{:S(2)}, u32[]{:S(2)}) collective-permute-start(f32[1,8,6912]{2,0,1:T(1,128)} %slice_bitcast_fusion.1), channel_id=1, source_target_pairs={{16,0},{17,1},{18,2},{19,3},{20,4},{21,5},{22,6},{23,7},{24,8},{25... | collective-permute-start | bytes 663560 | tf_op jit(solution)/shard_map/ppermute | solution.py:32
  16.6 195.5 %collective-permute-start.1 = (f32[1,16,6912]{2,1,0:T(8,128)}, f32[1,16,6912]{2,1,0:T(8,128)}, u32[]{:S(2)}, u32[]{:S(2)}) collective-permute-start(f32[1,16,6912]{2,1,0:T(8,128)} %copy.216), channel_id=1, source_target_pairs={{32,0},{64,32},{96,64},{33,1},{65,33},{97,65},{34,2},{66,34},{98,6... | collective-permute-start | bytes 1327112 | tf_op jit(solution)/shard_map/ppermute | solution.py:32
  204.7 14.4 %copy-start.97 = (f32[8]{0:T(128)S(1)}, f32[8]{0:T(128)}, u32[]{:S(2)}) copy-start(f32[8]{0:T(128)} %broadcast_select_fusion.14) | copy-start | bytes 100
  204.7 14.6 %copy-start.25 = (f32[1,8,2,6912]{3,2,1,0:T(2,128)S(1)}, f32[1,8,2,6912]{3,2,1,0:T(2,128)}, u32[]{:S(2)}) copy-start(f32[1,8,2,6912]{3,2,1,0:T(2,128)} %copy-done.24) | copy-start | bytes 1327108
  208.5 11.6 %copy-start.17 = (f32[1,8,2,6912]{3,0,2,1:T(1,128)S(1)}, f32[1,8,2,6912]{3,0,2,1:T(1,128)}, u32[]{:S(2)}) copy-start(f32[1,8,2,6912]{3,0,2,1:T(1,128)} %copy-done.16) | copy-start | bytes 1327108
  209.2 20.8 %copy-start.101 = (f32[8]{0:T(128)}, f32[8]{0:T(128)S(1)}, u32[]{:S(2)}) copy-start(f32[8]{0:T(128)S(1)} %add_multiply_fusion) | copy-start | bytes 100
  210.7 8.3 %collective-permute-start.2 = (f32[1,8,6912]{2,0,1:T(1,128)S(1)}, f32[1,8,6912]{2,0,1:T(1,128)S(1)}, u32[]{:S(2)}, u32[]{:S(2)}) collective-permute-start(f32[1,8,6912]{2,0,1:T(1,128)S(1)} %get-tuple-element.83), channel_id=1, source_target_pairs={{0,16},{1,17},{2,18},{3,19},{4,20},{5,21},{6,22},{7,23},{8,24},{9,... | collective-permute-start | bytes 663560 | tf_op jit(solution)/shard_map/ppermute | solution.py:30
  212.2 16.3 %collective-permute-start = (f32[1,16,6912]{2,1,0:T(8,128)S(1)}, f32[1,16,6912]{2,1,0:T(8,128)S(1)}, u32[]{:S(2)}, u32[]{:S(2)}) collective-permute-start(f32[1,16,6912]{2,1,0:T(8,128)S(1)} %get-tuple-element.79), channel_id=1, source_target_pairs={{0,32},{32,64},{64,96},{1,33},{33,65},{65,97},{2,34},{34,66},{66,9... | collective-permute-start | bytes 1327112 | tf_op jit(solution)/shard_map/ppermute | solution.py:30
  230.8 14.5 %copy-start.94 = (f32[8,1,1,1]{0,1,3,2:T(1,128)S(1)}, f32[8,1,1,1]{0,1,3,2:T(1,128)}, u32[]{:S(2)}) copy-start(f32[8,1,1,1]{0,1,3,2:T(1,128)} %constant.167) | copy-start | bytes 100
  249.3 33.0 %copy-start.12 = (f32[1,8,2,6912]{3,0,2,1:T(1,128)}, f32[1,8,2,6912]{3,0,2,1:T(1,128)S(1)}, u32[]{:S(2)}) copy-start(f32[1,8,2,6912]{3,0,2,1:T(1,128)S(1)} %fusion.95) | copy-start | bytes 1327108
  253.3 25.7 %copy-start.14 = (f32[1,8,2,6912]{3,0,2,1:T(1,128)}, f32[1,8,2,6912]{3,0,2,1:T(1,128)S(1)}, u32[]{:S(2)}) copy-start(f32[1,8,2,6912]{3,0,2,1:T(1,128)S(1)} %fusion.93) | copy-start | bytes 1327108
  260.7 17.5 %copy-start.10 = (f32[1,16,6912]{2,0,1:T(1,128)}, f32[1,16,6912]{2,0,1:T(1,128)S(1)}, u32[]{:S(2)}) copy-start(f32[1,16,6912]{2,0,1:T(1,128)S(1)} %fusion.163) | copy-start | bytes 1327108
  280.1 131.6 %collective-permute-start.7 = (f32[1,8,6912]{2,0,1:T(1,128)}, f32[1,8,6912]{2,0,1:T(1,128)}, u32[]{:S(2)}, u32[]{:S(2)}) collective-permute-start(f32[1,8,6912]{2,0,1:T(1,128)} %slice_bitcast_fusion), channel_id=1, source_target_pairs={{16,0},{17,1},{18,2},{19,3},{20,4},{21,5},{22,6},{23,7},{24,8},{25... | collective-permute-start | bytes 663560 | tf_op jit(solution)/shard_map/ppermute | solution.py:32
  283.3 131.5 %collective-permute-start.5 = (f32[1,16,6912]{2,1,0:T(8,128)}, f32[1,16,6912]{2,1,0:T(8,128)}, u32[]{:S(2)}, u32[]{:S(2)}) collective-permute-start(f32[1,16,6912]{2,1,0:T(8,128)} %copy.215), channel_id=1, source_target_pairs={{32,0},{64,32},{96,64},{33,1},{65,33},{97,65},{34,2},{66,34},{98,6... | collective-permute-start | bytes 1327112 | tf_op jit(solution)/shard_map/ppermute | solution.py:32
  411.0 13.6 %copy-start.13 = (f32[1,8,2,6912]{3,0,2,1:T(1,128)S(1)}, f32[1,8,2,6912]{3,0,2,1:T(1,128)}, u32[]{:S(2)}) copy-start(f32[1,8,2,6912]{3,0,2,1:T(1,128)} %copy-done.12) | copy-start | bytes 1327108
  411.0 13.6 %copy-start.15 = (f32[1,8,2,6912]{3,0,2,1:T(1,128)S(1)}, f32[1,8,2,6912]{3,0,2,1:T(1,128)}, u32[]{:S(2)}) copy-start(f32[1,8,2,6912]{3,0,2,1:T(1,128)} %copy-done.14) | copy-start | bytes 1327108
  413.2 11.9 %copy-start.38 = (f32[6912]{0:T(1024)S(1)}, f32[6912]{0:T(1024)}, u32[]{:S(2)}) copy-start(f32[6912]{0:T(1024)} %get-tuple-element.86) | copy-start | bytes 82948
  413.2 11.9 %copy-start.52 = (f32[8,8,1,1]{1,0,3,2:T(8,128)S(1)}, f32[8,8,1,1]{1,0,3,2:T(8,128)}, u32[]{:S(2)}) copy-start(f32[8,8,1,1]{1,0,3,2:T(8,128)} %constant.166) | copy-start | bytes 772
  413.3 11.9 %copy-start.90 = (f32[8]{0:T(128)S(1)}, f32[8]{0:T(128)}, u32[]{:S(2)}) copy-start(f32[8]{0:T(128)} %constant.131.clone) | copy-start | bytes 100
  413.3 11.9 %copy-start.92 = (f32[8]{0:T(128)S(1)}, f32[8]{0:T(128)}, u32[]{:S(2)}) copy-start(f32[8]{0:T(128)} %constant.130.clone) | copy-start | bytes 100
  413.3 8.4 %collective-permute-start.6 = (f32[1,8,6912]{2,0,1:T(1,128)S(1)}, f32[1,8,6912]{2,0,1:T(1,128)S(1)}, u32[]{:S(2)}, u32[]{:S(2)}) collective-permute-start(f32[1,8,6912]{2,0,1:T(1,128)S(1)} %get-tuple-element.77), channel_id=1, source_target_pairs={{0,16},{1,17},{2,18},{3,19},{4,20},{5,21},{6,22},{7,23},{8,24},{9,... | collective-permute-start | bytes 663560 | tf_op jit(solution)/shard_map/ppermute | solution.py:30
  415.8 18.2 %collective-permute-start.4 = (f32[1,16,6912]{2,1,0:T(8,128)S(1)}, f32[1,16,6912]{2,1,0:T(8,128)S(1)}, u32[]{:S(2)}, u32[]{:S(2)}) collective-permute-start(f32[1,16,6912]{2,1,0:T(8,128)S(1)} %get-tuple-element.73), channel_id=1, source_target_pairs={{0,32},{32,64},{64,96},{1,33},{33,65},{65,97},{2,34},{34,66},{66,9... | collective-permute-start | bytes 1327112 | tf_op jit(solution)/shard_map/ppermute | solution.py:30
  448.9 44.8 %copy-start.5 = (f32[8,16,6912]{2,1,0:T(8,128)}, f32[8,16,6912]{2,1,0:T(8,128)S(1)}, u32[]{:S(2)}) copy-start(f32[8,16,6912]{2,1,0:T(8,128)S(1)} %copy.117) | copy-start | bytes 10616836
  (91 other events, 326.6 us)
where the time goes:
time: 547 us; the launch traced here: 537 us
  blocking collectives  210 us (38%)
  local copies, waits for them, and re-layouts  142 us (26%)
  matrix products  116 us (21%)
  other arithmetic  37.9 us (7%)
  starting transfers between devices  16.4 us (3%)
  waiting for transfers between devices  9.67 us (2%)
    psum x5, blocking collectives, gather_moments(): integral_sums_table, bound_sums = lax.psum((partials, bound_sums), 'vert')  177 us
    psum x1, blocking collectives, gather_moments(): conduction_integral = lax.psum(heat_local, 'vert')  33.2 us
    dot_general x2, matrix products, advance(): jnp.einsum('ij,ejzv->eizv', derivative, grouped, precision=HIGHEST_PRECIS...  25.6 us
    unnamed x231, local copies, waits for them, and re-layouts  20.8 us
    slice x4, local copies, waits for them, and re-layouts, shift_velocity(): shifted = jnp.concatenate([field_entries[..., offset:], padding], -1)  16.2 us
    dot_general x3, matrix products, gather_moments(): jnp.dot(weighted, heat_basis, precision=HIGHEST_PRECISION, preferred_elem...  15.2 us
    dot_general x3, matrix products, gather_moments(): jnp.dot(flat, moment_basis, precision=HIGHEST_PRECISION, preferred_elemen...  12.6 us
  transfers between devices with their start and end apart: 8, of which 2 were waited for; matrix products, arithmetic and copies ran while one was open for 38% of the time, Pallas kernels for 0%

commit v1 on v0

--- a/solution.py
+++ b/solution.py
@@ -234,7 +234,7 @@
             weighted, heat_basis, precision=HIGHEST_PRECISION, preferred_element_type=jnp.float32
         )
         heat_local = 0.5 * (heat_parts[:, :3] - bulk_velocity * heat_parts[:, 3:4])
-        conduction_integral = lax.psum(heat_local, "vert")
+        conduction_integral = jax.lax.all_gather(heat_local, "vert").sum(axis=0)
         fluid_observables = (
             particle_concentration,
             bulk_velocity[:, 0],

time: 547 us -> 509 us (0.931)
  the two profiles are of different devices: /device:TPU:27 before, /device:TPU:31 now
where the time goes in v1:
time: 509 us; the launch traced here: 499 us
  blocking collectives  174 us (34%)
  local copies, waits for them, and re-layouts  140 us (28%)
  matrix products  117 us (23%)
  other arithmetic  36.7 us (7%)
  starting transfers between devices  16.6 us (3%)
  waiting for transfers between devices  10.8 us (2%)
    psum x3, blocking collectives, gather_moments(): integral_sums_table, bound_sums = lax.psum((partials, bound_sums), 'vert')  88.7 us
    all_gather x3, blocking collectives, gather_moments(): conduction_integral = jax.lax.all_gather(heat_local, 'vert').sum(axis=0)  85.1 us
    dot_general x2, matrix products, advance(): jnp.einsum('ij,ejzv->eizv', derivative, grouped, precision=HIGHEST_PRECIS...  25.6 us
    unnamed x233, local copies, waits for them, and re-layouts  20.8 us
    slice x4, local copies, waits for them, and re-layouts, shift_velocity(): shifted = jnp.concatenate([field_entries[..., offset:], padding], -1)  16.2 us
    dot_general x3, matrix products, gather_moments(): jnp.dot(weighted, heat_basis, precision=HIGHEST_PRECISION, preferred_elem...  15.2 us
    dot_general x3, matrix products, gather_moments(): jnp.dot(flat, moment_basis, precision=HIGHEST_PRECISION, preferred_elemen...  12.7 us
    ppermute x4, starting transfers between devices, with_halo(): lax.ppermute(head, axis, [((i + 1) % count, i) for i in range(ends)])  10.8 us
  transfers between devices with their start and end apart: 8, of which 2 were waited for; matrix products, arithmetic and copies ran while one was open for 41% of the time, Pallas kernels for 0%

profile of v1, /device:TPU:31, one launch (start us, length us, event | category | flops | bytes accessed | tf_op | source)
XLA Modules:
  0.0 499.0 jit_solution(7450444051594437957)
XLA Ops:
  0.7 5.3 %fusion.58 = f32[1,8,2,6912]{3,0,2,1:T(1,128)S(1)} fusion(f32[8,1,1,1]{0,1,3,2:T(1,128)} %constant.168, f32[8,16,6912]{2,1,0:T(8,128)} %param.12), kind=kOutput, calls=%fused_computation.74 | convolution fusion | flops 10616832 | bytes 3981344 | tf_op jit(solution)/shard_map/j,rejv->rev/dot_general | solution.py:291
  10.3 5.0 %fusion.150 = f32[1,16,6912]{2,0,1:T(1,128)S(1)} fusion(f32[8,1,1]{0,1,2:T(1,128)S(1)} %copy-done.56, f32[8,16,6912]{2,1,0:T(8,128)S(1)} %copy-done), kind=kOutput, calls=%fused_computation.308 | convolution fusion | flops 10616832 | bytes 3981344 | tf_op jit(solution)/shard_map/j,ejzv->ezv/dot_general | solution.py:265
  25.9 5.5 %fusion.148 = f32[1,16,6912]{2,0,1:T(1,128)} fusion(f32[8,1,1]{0,1,2:T(1,128)S(1)} %copy-done.53, f32[8,16,6912]{2,1,0:T(8,128)S(1)} %copy-done), kind=kOutput, calls=%fused_computation.306 | convolution fusion | flops 10616832 | bytes 3981344 | tf_op jit(solution)/shard_map/j,ejzv->ezv/dot_general | solution.py:264
  31.5 4.1 fusion.158
  35.5 4.1 fusion.157
  62.9 4.4 convolution_bitcast_fusion.4
  67.9 30.8 %all-reduce.10 = (f32[2,8]{1,0:T(2,128)}, f32[128,5]{0,1:T(8,128)}) all-reduce(f32[2,8]{1,0:T(2,128)} %pad_maximum_fusion.1, f32[128,5]{0,1:T(8,128)} %convolution_bitcast_fusion.4), channel_id=1, replica_groups=mesh['row'=4,'gz'=2,'vert'=16] {'vert'}, use_global_device_ids=true, to_apply=%region_4.5 | all-reduce | flops 656 | bytes 5248 | tf_op jit(solution)/shard_map/psum | solution.py:212
  104.9 4.7 fusion.83
  131.4 29.8 %all-gather = f32[2048,3]{0,1:T(4,128)S(1)} all-gather(f32[128,3]{0,1:T(4,128)} %subtract_multiply_fusion.14), channel_id=2, replica_groups=mesh['row'=4,'gz'=2,'vert'=16] {'vert'}, dimensions={0}, use_global_device_ids=true | all-gather | bytes 26112 | tf_op jit(solution)/shard_map/all_gather | solution.py:237
  184.3 4.2 copy.210
  201.8 5.9 %collective-permute-done.2 = f32[1,8,6912]{2,0,1:T(1,128)S(1)} collective-permute-done((f32[1,8,6912]{2,0,1:T(1,128)S(1)}, f32[1,8,6912]{2,0,1:T(1,128)S(1)}, u32[]{:S(2)}, u32[]{:S(2)}) %collective-permute-start.2) | collective-permute-done | bytes 221216 | tf_op jit(solution)/shard_map/ppermute | solution.py:30
  219.4 14.4 %fusion.23 = f32[8,16,6912]{2,0,1:T(8,128)S(1)} fusion(f32[8,16,6912]{2,0,1:T(8,128)} %bitcast.327, f32[8,8,1]{1,0,2:T(8,128)S(1)} %copy-done.106, f32[8,16,6911]{2,0,1:T(8,128)S(1)} %copy.209, f32[8,16,6911]{2,0,1:T(8,128)S(1)} %copy.210, f32[8,16,6864]{2,0,1:T(8,128)} %copy.211, f32[8,16,6864]{2,0,1:T(8,128)S(1)} %copy.212, f32[8]{0:T(128)S(1)} %add_multiply_fusion, ...), kind=kOutput, calls=%fused_computation.27 | convolution fusion | flops 124747776 | bytes 25806688 | tf_op jit(solution)/shard_map/ij,ejzv->eizv/dot_general | solution.py:263
  241.9 4.3 fusion.164
  258.7 4.1 fusion.154
  282.3 5.4 %fusion.162 = f32[128,5]{0,1:T(8,128)} fusion(f32[128,6912]{1,0:T(8,128)} %bitcast.324, f32[6912,5]{0,1:T(8,128)} %stack.24), kind=kOutput, calls=%fused_computation.320 | convolution fusion | flops 53084160 | bytes 3679744 | tf_op jit(solution)/shard_map/dot_general | solution.py:209
  288.9 29.3 %all-reduce.9 = (f32[2,8]{1,0:T(2,128)}, f32[128,5]{0,1:T(8,128)}) all-reduce(f32[2,8]{1,0:T(2,128)} %pad_maximum_fusion.2, f32[128,5]{0,1:T(8,128)} %fusion.162), channel_id=1, replica_groups=mesh['row'=4,'gz'=2,'vert'=16] {'vert'}, use_global_device_ids=true, to_apply=%region_8.9 | all-reduce | flops 656 | bytes 5248 | tf_op jit(solution)/shard_map/psum | solution.py:212
  322.6 5.9 %fusion.73 = f32[128,4]{0,1:T(4,128)S(1)} fusion(f32[128,6912]{1,0:T(8,128)} %bitcast.325, f32[128]{0:T(128)S(1)} %get-tuple-element.110, f32[128]{0:T(128)S(1)} %get-tuple-element.109, f32[128]{0:T(128)S(1)} %get-tuple-element.108, f32[6912]{0:T(1024)} %sub.385, f32[6912]{0:T(1024)} %sub.380, f32[6912]{0:T(1024)} %sub.375, f32[6912,1]{0,1:T(1,128)} %broadcast.609, ...), kind=kOutput, calls=%fused_computation.89 | convolution fusion | flops 50512896 | bytes 3736064 | tf_op jit(solution)/shard_map/dot_general | solution.py:233
  350.3 27.5 %all-gather.1 = f32[2048,3]{0,1:T(4,128)S(1)} all-gather(f32[128,3]{0,1:T(4,128)} %subtract_multiply_fusion.13), channel_id=3, replica_groups=mesh['row'=4,'gz'=2,'vert'=16] {'vert'}, dimensions={0}, use_global_device_ids=true | all-gather | bytes 26112 | tf_op jit(solution)/shard_map/all_gather | solution.py:237
  392.5 4.8 collective-permute-done.6
  400.9 4.8 fusion.2
  412.3 11.2 %fusion.18 = f32[8,16,6912]{2,0,1:T(8,128)S(1)} fusion(f32[8,16,6912]{2,0,1:T(8,128)S(1)} %fusion.23, f32[8,16,6912]{2,0,1:T(8,128)} %bitcast.326, f32[8,8,1]{1,0,2:T(8,128)S(1)} %copy-done.107, f32[8,16,6911]{2,0,1:T(8,128)} %get-tuple-element.57, f32[8,16,6911]{2,0,1:T(8,128)S(1)} %copy-done.22, f32[8,16,6864]{2,0,1:T(8,128)S(1)} %copy-done.21, ...), kind=kOutput, calls=%fused_computation.22 | convolution fusion | flops 124747776 | bytes 25806688 | tf_op jit(solution)/shard_map/ij,ejzv->eizv/dot_general | solution.py:263
  433.5 28.6 %all-reduce.8 = (f32[128,5]{0,1:T(8,128)S(1)}, f32[2,8]{1,0:T(2,128)S(1)}) all-reduce(f32[128,5]{0,1:T(8,128)S(1)} %fusion.165, f32[2,8]{1,0:T(2,128)S(1)} %pad_maximum_fusion.3), channel_id=1, replica_groups=mesh['row'=4,'gz'=2,'vert'=16] {'vert'}, use_global_device_ids=true, to_apply=%region_9.10 | all-reduce | flops 656 | bytes 5248 | tf_op jit(solution)/shard_map/psum | solution.py:212
  463.2 4.7 fusion.63
  469.7 27.9 %all-gather.2 = f32[2048,3]{0,1:T(4,128)S(1)} all-gather(f32[128,3]{0,1:T(4,128)S(1)} %subtract_multiply_fusion.12), channel_id=4, replica_groups=mesh['row'=4,'gz'=2,'vert'=16] {'vert'}, dimensions={0}, use_global_device_ids=true | all-gather | bytes 26112 | tf_op jit(solution)/shard_map/all_gather | solution.py:237
  (404 shorter events, 218.3 us)
Async XLA Ops:
  7.1 16.6 %copy-start.53 = (f32[8,1,1]{0,1,2:T(1,128)S(1)}, f32[8,1,1]{0,1,2:T(1,128)}, u32[]{:S(2)}) copy-start(f32[8,1,1]{0,1,2:T(1,128)} %constant.165) | copy-start | bytes 100
  7.1 190.2 %collective-permute-start.3 = (f32[1,8,6912]{2,0,1:T(1,128)}, f32[1,8,6912]{2,0,1:T(1,128)}, u32[]{:S(2)}, u32[]{:S(2)}) collective-permute-start(f32[1,8,6912]{2,0,1:T(1,128)} %slice_bitcast_fusion.1), channel_id=1, source_target_pairs={{16,0},{17,1},{18,2},{19,3},{20,4},{21,5},{22,6},{23,7},{24,8},{25... | collective-permute-start | bytes 663560 | tf_op jit(solution)/shard_map/ppermute | solution.py:32
  16.9 183.3 %collective-permute-start.1 = (f32[1,16,6912]{2,1,0:T(8,128)}, f32[1,16,6912]{2,1,0:T(8,128)}, u32[]{:S(2)}, u32[]{:S(2)}) collective-permute-start(f32[1,16,6912]{2,1,0:T(8,128)} %copy.222), channel_id=1, source_target_pairs={{32,0},{64,32},{96,64},{33,1},{65,33},{97,65},{34,2},{66,34},{98,6... | collective-permute-start | bytes 1327112 | tf_op jit(solution)/shard_map/ppermute | solution.py:32
  192.7 14.9 %copy-start.98 = (f32[8]{0:T(128)S(1)}, f32[8]{0:T(128)}, u32[]{:S(2)}) copy-start(f32[8]{0:T(128)} %broadcast_select_fusion.14) | copy-start | bytes 100
  192.7 15.2 %copy-start.25 = (f32[1,8,2,6912]{3,2,1,0:T(2,128)S(1)}, f32[1,8,2,6912]{3,2,1,0:T(2,128)}, u32[]{:S(2)}) copy-start(f32[1,8,2,6912]{3,2,1,0:T(2,128)} %copy-done.24) | copy-start | bytes 1327108
  196.5 12.1 %copy-start.17 = (f32[1,8,2,6912]{3,0,2,1:T(1,128)S(1)}, f32[1,8,2,6912]{3,0,2,1:T(1,128)}, u32[]{:S(2)}) copy-start(f32[1,8,2,6912]{3,0,2,1:T(1,128)} %copy-done.16) | copy-start | bytes 1327108
  197.3 21.3 %copy-start.102 = (f32[8]{0:T(128)}, f32[8]{0:T(128)S(1)}, u32[]{:S(2)}) copy-start(f32[8]{0:T(128)S(1)} %add_multiply_fusion) | copy-start | bytes 100
  198.8 8.9 %collective-permute-start.2 = (f32[1,8,6912]{2,0,1:T(1,128)S(1)}, f32[1,8,6912]{2,0,1:T(1,128)S(1)}, u32[]{:S(2)}, u32[]{:S(2)}) collective-permute-start(f32[1,8,6912]{2,0,1:T(1,128)S(1)} %get-tuple-element.83), channel_id=1, source_target_pairs={{0,16},{1,17},{2,18},{3,19},{4,20},{5,21},{6,22},{7,23},{8,24},{9,... | collective-permute-start | bytes 663560 | tf_op jit(solution)/shard_map/ppermute | solution.py:30
  200.3 16.8 %collective-permute-start = (f32[1,16,6912]{2,1,0:T(8,128)S(1)}, f32[1,16,6912]{2,1,0:T(8,128)S(1)}, u32[]{:S(2)}, u32[]{:S(2)}) collective-permute-start(f32[1,16,6912]{2,1,0:T(8,128)S(1)} %get-tuple-element.79), channel_id=1, source_target_pairs={{0,32},{32,64},{64,96},{1,33},{33,65},{65,97},{2,34},{34,66},{66,9... | collective-permute-start | bytes 1327112 | tf_op jit(solution)/shard_map/ppermute | solution.py:30
  219.4 14.5 %copy-start.94 = (f32[8,1,1,1]{0,1,3,2:T(1,128)S(1)}, f32[8,1,1,1]{0,1,3,2:T(1,128)}, u32[]{:S(2)}) copy-start(f32[8,1,1,1]{0,1,3,2:T(1,128)} %constant.167) | copy-start | bytes 100
  237.9 32.9 %copy-start.12 = (f32[1,8,2,6912]{3,0,2,1:T(1,128)}, f32[1,8,2,6912]{3,0,2,1:T(1,128)S(1)}, u32[]{:S(2)}) copy-start(f32[1,8,2,6912]{3,0,2,1:T(1,128)S(1)} %fusion.95) | copy-start | bytes 1327108
  241.9 25.7 %copy-start.14 = (f32[1,8,2,6912]{3,0,2,1:T(1,128)}, f32[1,8,2,6912]{3,0,2,1:T(1,128)S(1)}, u32[]{:S(2)}) copy-start(f32[1,8,2,6912]{3,0,2,1:T(1,128)S(1)} %fusion.93) | copy-start | bytes 1327108
  249.3 17.4 %copy-start.10 = (f32[1,16,6912]{2,0,1:T(1,128)}, f32[1,16,6912]{2,0,1:T(1,128)S(1)}, u32[]{:S(2)}) copy-start(f32[1,16,6912]{2,0,1:T(1,128)S(1)} %fusion.163) | copy-start | bytes 1327108
  268.7 118.3 %collective-permute-start.7 = (f32[1,8,6912]{2,0,1:T(1,128)}, f32[1,8,6912]{2,0,1:T(1,128)}, u32[]{:S(2)}, u32[]{:S(2)}) collective-permute-start(f32[1,8,6912]{2,0,1:T(1,128)} %slice_bitcast_fusion), channel_id=1, source_target_pairs={{16,0},{17,1},{18,2},{19,3},{20,4},{21,5},{22,6},{23,7},{24,8},{25... | collective-permute-start | bytes 663560 | tf_op jit(solution)/shard_map/ppermute | solution.py:32
  271.8 118.1 %collective-permute-start.5 = (f32[1,16,6912]{2,1,0:T(8,128)}, f32[1,16,6912]{2,1,0:T(8,128)}, u32[]{:S(2)}, u32[]{:S(2)}) collective-permute-start(f32[1,16,6912]{2,1,0:T(8,128)} %copy.221), channel_id=1, source_target_pairs={{32,0},{64,32},{96,64},{33,1},{65,33},{97,65},{34,2},{66,34},{98,6... | collective-permute-start | bytes 1327112 | tf_op jit(solution)/shard_map/ppermute | solution.py:32
  386.2 14.0 %copy-start.13 = (f32[1,8,2,6912]{3,0,2,1:T(1,128)S(1)}, f32[1,8,2,6912]{3,0,2,1:T(1,128)}, u32[]{:S(2)}) copy-start(f32[1,8,2,6912]{3,0,2,1:T(1,128)} %copy-done.12) | copy-start | bytes 1327108
  386.2 14.0 %copy-start.15 = (f32[1,8,2,6912]{3,0,2,1:T(1,128)S(1)}, f32[1,8,2,6912]{3,0,2,1:T(1,128)}, u32[]{:S(2)}) copy-start(f32[1,8,2,6912]{3,0,2,1:T(1,128)} %copy-done.14) | copy-start | bytes 1327108
  388.4 12.4 %copy-start.38 = (f32[6912]{0:T(1024)S(1)}, f32[6912]{0:T(1024)}, u32[]{:S(2)}) copy-start(f32[6912]{0:T(1024)} %get-tuple-element.86) | copy-start | bytes 82948
  388.5 12.4 %copy-start.52 = (f32[8,8,1,1]{1,0,3,2:T(8,128)S(1)}, f32[8,8,1,1]{1,0,3,2:T(8,128)}, u32[]{:S(2)}) copy-start(f32[8,8,1,1]{1,0,3,2:T(8,128)} %constant.166) | copy-start | bytes 772
  388.5 12.4 %copy-start.90 = (f32[8]{0:T(128)S(1)}, f32[8]{0:T(128)}, u32[]{:S(2)}) copy-start(f32[8]{0:T(128)} %constant.131.clone) | copy-start | bytes 100
  388.5 12.4 %copy-start.92 = (f32[8]{0:T(128)S(1)}, f32[8]{0:T(128)}, u32[]{:S(2)}) copy-start(f32[8]{0:T(128)} %constant.130.clone) | copy-start | bytes 100
  388.5 8.9 %collective-permute-start.6 = (f32[1,8,6912]{2,0,1:T(1,128)S(1)}, f32[1,8,6912]{2,0,1:T(1,128)S(1)}, u32[]{:S(2)}, u32[]{:S(2)}) collective-permute-start(f32[1,8,6912]{2,0,1:T(1,128)S(1)} %get-tuple-element.77), channel_id=1, source_target_pairs={{0,16},{1,17},{2,18},{3,19},{4,20},{5,21},{6,22},{7,23},{8,24},{9,... | collective-permute-start | bytes 663560 | tf_op jit(solution)/shard_map/ppermute | solution.py:30
  391.0 18.8 %collective-permute-start.4 = (f32[1,16,6912]{2,1,0:T(8,128)S(1)}, f32[1,16,6912]{2,1,0:T(8,128)S(1)}, u32[]{:S(2)}, u32[]{:S(2)}) collective-permute-start(f32[1,16,6912]{2,1,0:T(8,128)S(1)} %get-tuple-element.73), channel_id=1, source_target_pairs={{0,32},{32,64},{64,96},{1,33},{33,65},{65,97},{2,34},{34,66},{66,9... | collective-permute-start | bytes 1327112 | tf_op jit(solution)/shard_map/ppermute | solution.py:30
  424.6 38.6 %copy-start.5 = (f32[8,16,6912]{2,1,0:T(8,128)}, f32[8,16,6912]{2,1,0:T(8,128)S(1)}, u32[]{:S(2)}) copy-start(f32[8,16,6912]{2,1,0:T(8,128)S(1)} %copy.117) | copy-start | bytes 10616836
  (92 other events, 335.8 us)
